TPU v7x, 32 devices: a whole 2x2x4 slice. The times are simulated.
32 devices in a mesh: chip: 2 (over core), row: 4 (over y, x), grp: 4 (over z).
Axes of the slice: x: 2, y: 2, z: 4, core: 2. Of those that a mesh axis runs over, the one named last changes fastest.
Arguments:
- old_velocity: float32 [2, 1024, 2048], P(None, 'row', ('chip', 'grp')), may hold values from -6 to 6
- surface_stress: float32 [2, 1024, 2048], P(None, 'row', ('chip', 'grp')), may hold values from -6 to 6
- mass_term: float32 [1024, 2048], P('row', ('chip', 'grp')), may hold values from 0.2 to 2
- ocean_drag: float32 [1024, 2048], P('row', ('chip', 'grp')), may hold values from 0.1 to 1
- strength: float32 [1024, 2048], P('row', ('chip', 'grp')), may hold values from 1 to 10
- ice_mask: int32 [1024, 2048], P('row', ('chip', 'grp')), may hold values from 0 to 1, as said below
- ocean_mask: int32 [1024, 2048], P('row', ('chip', 'grp')), may hold values 0 or 1
- ice_blocks: int32 [8, 8], P(('chip', 'grp')), may hold values from 0 to 15, as said below
Outputs:
- new_velocity: float32 [2, 1024, 2048], P(None, 'row', ('chip', 'grp'))
Inputs may be any that keep to these rules, and one draw needn't show every extreme that they name: `ice_blocks`: entry n of row c names block n % 4 (row-major over the blocks of 128 x 128 cells of a tile) of tile row n // 4 in tile column c. Each row lists 8 different blocks; the blocks of one tile stand together, tiles with more listed blocks first; all 4 blocks of the last tile row of every column are listed. The entry at place k of a row is owned by tile row k % 4 of that column, as its block number k // 4. `ice_mask`: ice lies only in cells of the blocks listed in ice_blocks.
All inputs are finite; a program needn't handle non-finite values. No bound on the sum of `ocean_mask` on one device may be relied on, other than what follows from the above.
Results may differ from a plain program's by a relative error of at most 0.00011.
Values sent between devices are 32-bit elements; how exact they have to be, the bound alone decides.
A program may use at most 128 MiB of HBM per device.

v0:
```python
import jax
import jax.numpy as jnp
from jax import lax
from jax.sharding import PartitionSpec as P

BS = 128
KRYLOV = 2
CYCLES = 2
SWEEPS = 2


RELAX = 0.8
DMIN_SQ = 0.25


def extended(array, sides, width):
    for axis, dim in sides:
        size, length = (lax.axis_size(axis), array.shape[dim])
        up = [(i, (i + 1) % size) for i in range(size - 1)]
        down = [(j, i) for i, j in up]
        last = lax.slice_in_dim(array, length - width, length, axis=dim)
        initial = lax.slice_in_dim(array, 0, width, axis=dim)
        before = lax.ppermute(last, axis, up)
        after = lax.ppermute(initial, axis, down)
        array = jnp.concatenate([before, array, after], axis=dim)
    return array


def stencil(padded, zeta_field, diag_field):

    def pieces(field):
        center = field[..., 1:-1, 1:-1]
        second_x = field[..., 2:, 1:-1] + field[..., :-2, 1:-1] - 2.0 * center
        second_y = field[..., 1:-1, 2:] + field[..., 1:-1, :-2] - 2.0 * center
        mixed = 0.25 * (
            field[..., 2:, 2:] - field[..., 2:, :-2] - field[..., :-2, 2:] + field[..., :-2, :-2]
        )
        return (center, second_x, second_y, mixed)

    part_u = pieces(padded[..., 0, :, :])
    part_v = pieces(padded[..., 1, :, :])
    along_u = (
        diag_field * part_u[0]
        - 1.25 * zeta_field * part_u[1]
        - 0.25 * zeta_field * part_u[2]
        - zeta_field * part_v[3]
    )
    along_v = (
        diag_field * part_v[0]
        - 0.25 * zeta_field * part_v[1]
        - 1.25 * zeta_field * part_v[2]
        - zeta_field * part_u[3]
    )
    return jnp.stack([along_u, along_v], axis=-3)


def precondition(vector, zeta_blocks, diag_blocks):
    diagonal_total = (diag_blocks + 3.0 * zeta_blocks)[:, None]
    iterate = vector / diagonal_total
    for relaxation in range(SWEEPS):
        padded = jnp.pad(iterate, ((0, 0), (0, 0), (1, 1), (1, 1)))
        iterate = (
            iterate + RELAX * (vector - stencil(padded, zeta_blocks, diag_blocks)) / diagonal_total
        )
    return iterate


def least_squares(hessenberg, start_norm):
    steps_count = hessenberg.shape[1]
    row_list = [hessenberg[i] for i in range(steps_count + 1)]
    target_vec = [start_norm] + [jnp.zeros((), jnp.float32) for i in range(steps_count)]
    for j in range(steps_count):
        upper = row_list[j][j]
        lower = row_list[j + 1][j]
        radius = jnp.sqrt(upper * upper + lower * lower)
        cosine = upper / radius
        sine_part = lower / radius
        first_row = cosine * row_list[j] + sine_part * row_list[j + 1]
        second_row = -sine_part * row_list[j] + cosine * row_list[j + 1]
        row_list[j], row_list[j + 1] = (first_row, second_row)
        first_val = cosine * target_vec[j] + sine_part * target_vec[j + 1]
        second_val = -sine_part * target_vec[j] + cosine * target_vec[j + 1]
        target_vec[j], target_vec[j + 1] = (first_val, second_val)
    weights_out = [None] * steps_count
    for j in range(steps_count - 1, -1, -1):
        accum = target_vec[j]
        for i in range(j + 1, steps_count):
            accum = accum - row_list[j][i] * weights_out[i]
        weights_out[j] = accum / row_list[j][j]
    return weights_out


def grid_to_blocks(tile_grid):
    channels, tile_rows, tile_cols = tile_grid.shape
    shaped = tile_grid.reshape(channels, tile_rows // BS, BS, tile_cols // BS, BS).transpose(
        1, 3, 0, 2, 4
    )
    return shaped.reshape(tile_rows // BS * (tile_cols // BS), channels, BS * BS)


def blocks_to_grid(blocks, tile_rows, tile_cols):
    channels = blocks.shape[1]
    shaped = blocks.reshape(tile_rows // BS, tile_cols // BS, channels, BS, BS).transpose(
        2, 0, 3, 1, 4
    )
    return shaped.reshape(channels, tile_rows, tile_cols)


def select(matrix, blocks):
    return jnp.einsum("st,tcx->scx", matrix, blocks, precision=lax.Precision.HIGHEST)


def shards(
    old_velocity, surface_stress, mass_term, ocean_drag, strength, ice_mask, ocean_mask, ice_blocks
):
    tile_rows = old_velocity.shape[1]
    tile_cols = old_velocity.shape[2]
    tile_count = tile_rows // BS * (tile_cols // BS)
    padded = extended(old_velocity, (("row", 1), (("chip", "grp"), 2)), 1)
    flow_u = padded[0]
    flow_v = padded[1]
    strain_xx = 0.5 * (flow_u[2:, 1:-1] - flow_u[:-2, 1:-1])
    strain_yy = 0.5 * (flow_v[1:-1, 2:] - flow_v[1:-1, :-2])
    strain_xy = 0.25 * (flow_u[1:-1, 2:] - flow_u[1:-1, :-2] + flow_v[2:, 1:-1] - flow_v[:-2, 1:-1])
    deform_sq = (
        1.25 * (strain_xx * strain_xx + strain_yy * strain_yy)
        + strain_xy * strain_xy
        + 1.5 * strain_xx * strain_yy
    )
    is_ocean = ocean_mask.astype(jnp.float32)
    zeta_tile = (
        is_ocean * ice_mask.astype(jnp.float32) * strength / (2.0 * jnp.sqrt(deform_sq + DMIN_SQ))
    )
    diag_tile = is_ocean * (mass_term + ocean_drag) + (1.0 - is_ocean)
    rhs_tile = is_ocean * (surface_stress + mass_term * old_velocity)
    coef_blocks = grid_to_blocks(
        jnp.concatenate([zeta_tile[None], diag_tile[None], rhs_tile], axis=0)
    )
    row_count = lax.axis_size("row")
    my_row = lax.axis_index("row")
    listed = ice_blocks[0]
    list_len = listed.shape[0]
    capacity = (tile_count + row_count - 1) // row_count
    slot_count = list_len // row_count
    rank_list = jnp.arange(list_len, dtype=jnp.int32)
    owner_row = rank_list % row_count
    source = listed // tile_count
    inside = listed % tile_count
    earlier = (
        (source[None, :] == source[:, None])
        & (owner_row[None, :] == owner_row[:, None])
        & (rank_list[None, :] < rank_list[:, None])
    )
    position = jnp.sum(earlier.astype(jnp.int32), axis=1)
    target = owner_row * capacity + position
    from_me = (source == my_row).astype(jnp.float32)
    place_ids = jnp.arange(row_count * capacity, dtype=jnp.int32)
    pick_target = (target[:, None] == place_ids[None, :]).astype(jnp.float32) * from_me[:, None]
    pick_inside = (inside[:, None] == jnp.arange(tile_count, dtype=jnp.int32)[None, :]).astype(
        jnp.float32
    )
    send_matrix = jnp.dot(pick_target.T, pick_inside, precision=lax.Precision.HIGHEST)
    owned_ranks = my_row + row_count * jnp.arange(slot_count, dtype=jnp.int32)
    arrival = jnp.take(source * capacity + position, owned_ranks)
    receive_matrix = (arrival[:, None] == place_ids[None, :]).astype(jnp.float32)

    def tile_operator(tile_vector):
        tile_grid = blocks_to_grid(tile_vector, tile_rows, tile_cols)
        grown = extended(tile_grid, (("row", 1), (("chip", "grp"), 2)), 1)
        return grid_to_blocks(stencil(grown, zeta_tile, diag_tile))

    outgoing = select(send_matrix, coef_blocks)
    local_coef = select(
        receive_matrix, lax.all_to_all(outgoing, "row", split_axis=0, concat_axis=0, tiled=True)
    )
    rhs = local_coef[:, 2:4]

    def to_tiles(vector):
        returned = lax.all_to_all(
            select(receive_matrix.T, vector), "row", split_axis=0, concat_axis=0, tiled=True
        )
        return select(send_matrix.T, returned)

    def apply_system(vector):
        images = tile_operator(to_tiles(vector))
        return select(
            receive_matrix,
            lax.all_to_all(
                select(send_matrix, images), "row", split_axis=0, concat_axis=0, tiled=True
            ),
        )

    zeta_blocks = local_coef[:, 0].reshape(-1, BS, BS)
    diag_blocks = local_coef[:, 1].reshape(-1, BS, BS)
    solution = jnp.zeros_like(rhs)
    for restart in range(CYCLES):
        if restart == 0:
            residual = rhs
        else:
            residual = rhs - apply_system(solution)
        start_norm = jnp.sqrt(lax.psum(jnp.sum(residual * residual), ("chip", "row", "grp")))
        basis_list = [residual / start_norm]
        directions = []
        hessenberg = jnp.zeros((KRYLOV + 1, KRYLOV), jnp.float32)
        for arnoldi in range(KRYLOV):
            apply_vector = basis_list[arnoldi]
            shaped = apply_vector.reshape(apply_vector.shape[0], 2, BS, BS)
            direction = precondition(shaped, zeta_blocks, diag_blocks).reshape(apply_vector.shape)
            directions.append(direction)
            images = apply_system(direction)
            local_products = jnp.stack([jnp.sum(images * vector) for vector in basis_list])
            products, square = lax.psum(
                (local_products, jnp.sum(images * images)), ("chip", "row", "grp")
            )
            for i in range(arnoldi + 1):
                images = images - products[i] * basis_list[i]
            new_norm = jnp.sqrt(square - jnp.sum(products * products))
            hessenberg = (
                hessenberg.at[: arnoldi + 1, arnoldi]
                .set(products)
                .at[arnoldi + 1, arnoldi]
                .set(new_norm)
            )
            if arnoldi + 1 < KRYLOV:
                basis_list.append(images / new_norm)
        weights_out = least_squares(hessenberg, start_norm)
        for arnoldi in range(KRYLOV):
            solution = solution + weights_out[arnoldi] * directions[arnoldi]
    return blocks_to_grid(to_tiles(solution), tile_rows, tile_cols)


def solution(mesh):
    return jax.shard_map(
        shards,
        mesh=mesh,
        in_specs=(
            P(None, "row", ("chip", "grp")),
            P(None, "row", ("chip", "grp")),
            P("row", ("chip", "grp")),
            P("row", ("chip", "grp")),
            P("row", ("chip", "grp")),
            P("row", ("chip", "grp")),
            P("row", ("chip", "grp")),
            P(("chip", "grp"), None),
        ),
        out_specs=P(None, "row", ("chip", "grp")),
        check_vma=False,
    )
```

profile of v0, /device:TPU:0, one launch (start us, length us, event | category | flops | bytes accessed | tf_op | source)
XLA Modules:
  0.0 627.7 jit_solution(18288621775122642015)
XLA Ops:
  0.8 4.8 collective-permute-start
  11.3 3.5 collective-permute-start.2
  16.7 2.5 collective-permute-done.2
  19.2 7.0 %collective-permute-done.3 = f32[2,258,1]{2,1,0:T(8,128)S(1)} collective-permute-done((f32[2,258,1]{2,1,0:T(8,128)S(1)}, f32[2,258,1]{2,1,0:T(8,128)S(1)}, u32[]{:S(2)}, u32[]{:S(2)}) %collective-permute-start.3) | collective-permute-done | bytes 2096 | tf_op jit(solution)/shard_map/ppermute | solution.py:24
  29.3 2.3 fusion.2
  31.7 1.7 copy.105
  33.3 4.6 all-to-all-start
  38.6 13.7 %all-to-all-done = f32[4,4,16384]{2,1,0:T(4,128)S(1)} async-done(((f32[4,4,16384]{2,1,0:T(4,128)}), f32[4,4,16384]{2,1,0:T(4,128)S(1)}, u32[]{:S(2)}, u32[]{:S(2)}) %all-to-all-start) | async-done | bytes 1048608 | tf_op jit(solution)/shard_map/all_to_all | solution.py:174
  52.3 1.7 fusion
  54.9 38.8 %psum.70 = f32[]{:T(128)} all-reduce(f32[]{:T(128)} %multiply_reduce_fusion.11), channel_id=1, replica_groups=mesh['chip'=2,'row'=4,'grp'=4] {'chip','row','grp'}, use_global_device_ids=true, to_apply=%region_2.3 | all-reduce | flops 1 | bytes 8 | tf_op jit(solution)/shard_map/psum | solution.py:201
  99.0 11.6 %all_to_all.60 = f32[4,2,16384]{2,1,0:T(2,128)S(1)} all-to-all(f32[4,2,16384]{2,1,0:T(2,128)S(1)} %copy.107), channel_id=1, replica_groups=mesh['chip'=2,'row'=4,'grp'=4] {'row'}, dimensions={0} | all-to-all | bytes 1048576 | tf_op jit(solution)/shard_map/all_to_all | solution.py:179
  113.2 2.8 collective-permute-start.4
  117.4 4.2 collective-permute-done.5
  121.7 3.6 collective-permute-start.6
  126.6 4.3 collective-permute-done.6
  130.9 2.8 collective-permute-done.7
  137.5 11.0 %all_to_all.61 = f32[4,2,16384]{2,1,0:T(2,128)S(1)} all-to-all(f32[4,2,16384]{2,1,0:T(2,128)S(1)} %copy.114), channel_id=1, replica_groups=mesh['chip'=2,'row'=4,'grp'=4] {'row'}, dimensions={0} | all-to-all | bytes 1048576 | tf_op jit(solution)/shard_map/all_to_all | solution.py:188
  148.5 1.7 multiply_reduce_fusion.10
  150.3 38.5 %all-reduce.13 = (f32[]{:T(128)}, f32[1]{0:T(128)}) all-reduce(f32[]{:T(128)} %get-tuple-element.110, f32[1]{0:T(128)} %bitcast.21), channel_id=1, replica_groups=mesh['chip'=2,'row'=4,'grp'=4] {'chip','row','grp'}, use_global_device_ids=true, to_apply=%region_6.7 | all-reduce | flops 2 | bytes 16 | tf_op jit(solution)/shard_map/psum | solution.py:212
  196.0 11.3 %all_to_all.62 = f32[4,2,16384]{2,1,0:T(2,128)S(1)} all-to-all(f32[4,2,16384]{2,1,0:T(2,128)S(1)} %copy.116), channel_id=1, replica_groups=mesh['chip'=2,'row'=4,'grp'=4] {'row'}, dimensions={0} | all-to-all | bytes 1048576 | tf_op jit(solution)/shard_map/all_to_all | solution.py:179
  207.3 1.5 fusion.27
  211.8 2.8 collective-permute-start.8
  215.9 4.2 collective-permute-done.9
  220.3 3.7 collective-permute-start.10
  224.0 1.5 collective-permute-start.11
  225.5 4.2 collective-permute-done.10
  229.7 3.4 collective-permute-done.11
  237.7 3.8 all-to-all-start.4
  243.6 4.7 all-to-all-done.4
  248.2 1.8 multiply_reduce_fusion.6
  251.5 39.1 %all-reduce.12 = (f32[2]{0:T(128)S(1)}, f32[]{:T(128)}) all-reduce(f32[2]{0:T(128)S(1)} %pad_maximum_fusion.12, f32[]{:T(128)} %get-tuple-element.106), channel_id=1, replica_groups=mesh['chip'=2,'row'=4,'grp'=4] {'chip','row','grp'}, use_global_device_ids=true, to_apply=%region_10.11 | all-reduce | flops 3 | bytes 24 | tf_op jit(solution)/shard_map/psum | solution.py:212
  292.6 2.0 broadcast_select_fusion.1
  308.2 11.4 %all_to_all.63 = f32[4,2,16384]{2,1,0:T(2,128)S(1)} all-to-all(f32[4,2,16384]{2,1,0:T(2,128)S(1)} %copy.125), channel_id=1, replica_groups=mesh['chip'=2,'row'=4,'grp'=4] {'row'}, dimensions={0} | all-to-all | bytes 1048576 | tf_op jit(solution)/shard_map/all_to_all | solution.py:179
  319.6 1.5 fusion.21
  324.2 2.8 collective-permute-start.12
  328.3 4.2 collective-permute-done.13
  332.7 2.8 collective-permute-start.14
  335.4 1.7 collective-permute-start.15
  337.2 3.0 collective-permute-done.14
  340.2 4.3 collective-permute-done.15
  348.2 10.8 %all_to_all.64 = f32[4,2,16384]{2,1,0:T(2,128)S(1)} all-to-all(f32[4,2,16384]{2,1,0:T(2,128)S(1)} %copy.132), channel_id=1, replica_groups=mesh['chip'=2,'row'=4,'grp'=4] {'row'}, dimensions={0} | all-to-all | bytes 1048576 | tf_op jit(solution)/shard_map/all_to_all | solution.py:188
  359.1 1.7 multiply_reduce_fusion.5
  360.8 38.5 %psum.75 = f32[]{:T(128)} all-reduce(f32[]{:T(128)} %get-tuple-element.196), channel_id=1, replica_groups=mesh['chip'=2,'row'=4,'grp'=4] {'chip','row','grp'}, use_global_device_ids=true, to_apply=%region_15.16 | all-reduce | flops 1 | bytes 8 | tf_op jit(solution)/shard_map/psum | solution.py:201
  404.4 11.4 %all_to_all.65 = f32[4,2,16384]{2,1,0:T(2,128)S(1)} all-to-all(f32[4,2,16384]{2,1,0:T(2,128)S(1)} %copy.134), channel_id=1, replica_groups=mesh['chip'=2,'row'=4,'grp'=4] {'row'}, dimensions={0} | all-to-all | bytes 1048576 | tf_op jit(solution)/shard_map/all_to_all | solution.py:179
  420.4 2.8 collective-permute-start.16
  424.5 4.2 collective-permute-done.17
  428.9 3.4 collective-permute-start.18
  433.6 4.0 collective-permute-done.18
  437.6 3.5 collective-permute-done.19
  444.9 11.0 %all_to_all.66 = f32[4,2,16384]{2,1,0:T(2,128)S(1)} all-to-all(f32[4,2,16384]{2,1,0:T(2,128)S(1)} %copy.141), channel_id=1, replica_groups=mesh['chip'=2,'row'=4,'grp'=4] {'row'}, dimensions={0} | all-to-all | bytes 1048576 | tf_op jit(solution)/shard_map/all_to_all | solution.py:188
  455.9 1.7 multiply_reduce_fusion.4
  457.6 38.9 %all-reduce.11 = (f32[]{:T(128)}, f32[1]{0:T(128)}) all-reduce(f32[]{:T(128)} %get-tuple-element.105, f32[1]{0:T(128)} %bitcast.65), channel_id=1, replica_groups=mesh['chip'=2,'row'=4,'grp'=4] {'chip','row','grp'}, use_global_device_ids=true, to_apply=%region_19.20 | all-reduce | flops 2 | bytes 16 | tf_op jit(solution)/shard_map/psum | solution.py:212
  504.5 11.3 %all_to_all.67 = f32[4,2,16384]{2,1,0:T(2,128)S(1)} all-to-all(f32[4,2,16384]{2,1,0:T(2,128)S(1)} %copy.143), channel_id=1, replica_groups=mesh['chip'=2,'row'=4,'grp'=4] {'row'}, dimensions={0} | all-to-all | bytes 1048576 | tf_op jit(solution)/shard_map/all_to_all | solution.py:179
  518.5 2.8 collective-permute-start.20
  522.7 4.2 collective-permute-done.21
  527.0 3.2 collective-permute-start.22
  531.5 3.9 collective-permute-done.22
  535.4 3.9 collective-permute-done.23
  543.9 4.0 all-to-all-start.10
  548.9 5.7 all-to-all-done.10
  554.6 1.8 multiply_reduce_fusion
  557.6 38.7 %all-reduce.10 = (f32[2]{0:T(128)S(1)}, f32[]{:T(128)}) all-reduce(f32[2]{0:T(128)S(1)} %pad_maximum_fusion.13, f32[]{:T(128)} %get-tuple-element.101), channel_id=1, replica_groups=mesh['chip'=2,'row'=4,'grp'=4] {'chip','row','grp'}, use_global_device_ids=true, to_apply=%region_22.23 | all-reduce | flops 3 | bytes 24 | tf_op jit(solution)/shard_map/psum | solution.py:212
  598.1 2.0 broadcast_select_fusion
  612.3 11.4 %all_to_all.68 = f32[4,2,16384]{2,1,0:T(2,128)S(1)} all-to-all(f32[4,2,16384]{2,1,0:T(2,128)S(1)} %copy.152), channel_id=1, replica_groups=mesh['chip'=2,'row'=4,'grp'=4] {'row'}, dimensions={0} | all-to-all | bytes 1048576 | tf_op jit(solution)/shard_map/all_to_all | solution.py:179
  (280 shorter events, 101.0 us)
Async XLA Ops:
  0.0 8.6 %copy-start = (f32[2,256,256]{2,1,0:T(8,128)S(1)}, f32[2,256,256]{2,1,0:T(8,128)}, u32[]{:S(2)}) copy-start(f32[2,256,256]{2,1,0:T(8,128)} %param.24) | copy-start | bytes 1572868
  0.8 9.2 %collective-permute-start = (f32[2,1,256]{2,1,0:T(1,128)S(1)}, f32[2,1,256]{2,1,0:T(1,128)S(1)}, u32[]{:S(2)}, u32[]{:S(2)}) collective-permute-start(f32[2,1,256]{2,1,0:T(1,128)S(1)} %get-tuple-element.159), channel_id=1, source_target_pairs={{0,4},{4,8},{8,12},{1,5},{5,9},{9,13},{2,6},{6,10},{10,14},{3,7},{... | collective-permute-start | bytes 6152 | tf_op jit(solution)/shard_map/ppermute | solution.py:23
  5.6 5.5 collective-permute-start.1
  7.9 0.7 copy-start.16
  11.3 7.9 %collective-permute-start.2 = (f32[2,258,1]{2,1,0:T(8,128)S(1)}, f32[2,258,1]{2,1,0:T(8,128)S(1)}, u32[]{:S(2)}, u32[]{:S(2)}) collective-permute-start(f32[2,258,1]{2,1,0:T(8,128)S(1)} %get-tuple-element.145), channel_id=1, source_target_pairs={{0,1},{1,2},{2,3},{3,16},{16,17},{17,18},{18,19},{4,5},{5,6},{6,7}... | collective-permute-start | bytes 6200 | tf_op jit(solution)/shard_map/ppermute | solution.py:23
  14.8 11.4 %collective-permute-start.3 = (f32[2,258,1]{2,1,0:T(8,128)S(1)}, f32[2,258,1]{2,1,0:T(8,128)S(1)}, u32[]{:S(2)}, u32[]{:S(2)}) collective-permute-start(f32[2,258,1]{2,1,0:T(8,128)S(1)} %get-tuple-element.146), channel_id=1, source_target_pairs={{1,0},{2,1},{3,2},{16,3},{17,16},{18,17},{19,18},{5,4},{6,5},{7,6}... | collective-permute-start | bytes 6200 | tf_op jit(solution)/shard_map/ppermute | solution.py:24
  26.6 1.0 copy-start.11
  26.6 1.0 copy-start.12
  26.6 1.1 copy-start.13
  26.6 1.2 copy-start.14
  26.6 1.2 copy-start.15
  33.3 19.0 %all-to-all-start = ((f32[4,4,16384]{2,1,0:T(4,128)}), f32[4,4,16384]{2,1,0:T(4,128)S(1)}, u32[]{:S(2)}, u32[]{:S(2)}) async-start(f32[4,4,16384]{2,1,0:T(4,128)} %copy.105), calls=%async_computation | async-start | bytes 2097152 | tf_op jit(solution)/shard_map/all_to_all | solution.py:174
  94.5 0.7 copy-start.1
  113.2 4.1 collective-permute-start.4
  116.1 5.5 collective-permute-start.5
  121.7 9.2 %collective-permute-start.6 = (f32[2,258,1]{2,1,0:T(8,128)S(1)}, f32[2,258,1]{2,1,0:T(8,128)S(1)}, u32[]{:S(2)}, u32[]{:S(2)}) collective-permute-start(f32[2,258,1]{2,1,0:T(8,128)S(1)} %get-tuple-element.143), channel_id=1, source_target_pairs={{0,1},{1,2},{2,3},{3,16},{16,17},{17,18},{18,19},{4,5},{5,6},{6,7}... | collective-permute-start | bytes 6200 | tf_op jit(solution)/shard_map/ppermute | solution.py:23
  125.3 8.4 %collective-permute-start.7 = (f32[2,258,1]{2,1,0:T(8,128)S(1)}, f32[2,258,1]{2,1,0:T(8,128)S(1)}, u32[]{:S(2)}, u32[]{:S(2)}) collective-permute-start(f32[2,258,1]{2,1,0:T(8,128)S(1)} %get-tuple-element.144), channel_id=1, source_target_pairs={{1,0},{2,1},{3,2},{16,3},{17,16},{18,17},{19,18},{5,4},{6,5},{7,6}... | collective-permute-start | bytes 6200 | tf_op jit(solution)/shard_map/ppermute | solution.py:24
  137.5 11.0 %copy-start.2 = (f32[2,2,16384]{2,0,1:T(2,128)S(1)}, f32[2,2,16384]{2,0,1:T(2,128)}, u32[]{:S(2)}) copy-start(f32[2,2,16384]{2,0,1:T(2,128)} %copy-done.1) | copy-start | bytes 786436
  211.8 4.1 collective-permute-start.8
  214.6 5.5 collective-permute-start.9
  220.3 9.5 %collective-permute-start.10 = (f32[2,258,1]{2,1,0:T(8,128)S(1)}, f32[2,258,1]{2,1,0:T(8,128)S(1)}, u32[]{:S(2)}, u32[]{:S(2)}) collective-permute-start(f32[2,258,1]{2,1,0:T(8,128)S(1)} %get-tuple-element.141), channel_id=1, source_target_pairs={{0,1},{1,2},{2,3},{3,16},{16,17},{17,18},{18,19},{4,5},{5,6},{6,7}... | collective-permute-start | bytes 6200 | tf_op jit(solution)/shard_map/ppermute | solution.py:23
  224.0 9.1 %collective-permute-start.11 = (f32[2,258,1]{2,1,0:T(8,128)S(1)}, f32[2,258,1]{2,1,0:T(8,128)S(1)}, u32[]{:S(2)}, u32[]{:S(2)}) collective-permute-start(f32[2,258,1]{2,1,0:T(8,128)S(1)} %get-tuple-element.142), channel_id=1, source_target_pairs={{1,0},{2,1},{3,2},{16,3},{17,16},{18,17},{19,18},{5,4},{6,5},{7,6}... | collective-permute-start | bytes 6200 | tf_op jit(solution)/shard_map/ppermute | solution.py:24
  237.7 10.5 %copy-start.3 = (f32[2,2,16384]{2,0,1:T(2,128)S(1)}, f32[2,2,16384]{2,0,1:T(2,128)}, u32[]{:S(2)}) copy-start(f32[2,2,16384]{2,0,1:T(2,128)} %copy-done.1) | copy-start | bytes 786436
  237.7 10.5 %all-to-all-start.4 = ((f32[4,2,16384]{2,1,0:T(2,128)}), f32[4,2,16384]{2,1,0:T(2,128)S(1)}, u32[]{:S(2)}, u32[]{:S(2)}) async-start(f32[4,2,16384]{2,1,0:T(2,128)} %copy.123), calls=%async_computation.4 | async-start | bytes 1048576 | tf_op jit(solution)/shard_map/all_to_all | solution.py:188
  324.2 4.1 collective-permute-start.12
  327.0 5.5 collective-permute-start.13
  332.7 7.5 %collective-permute-start.14 = (f32[2,258,1]{2,1,0:T(8,128)S(1)}, f32[2,258,1]{2,1,0:T(8,128)S(1)}, u32[]{:S(2)}, u32[]{:S(2)}) collective-permute-start(f32[2,258,1]{2,1,0:T(8,128)S(1)} %get-tuple-element.139), channel_id=1, source_target_pairs={{0,1},{1,2},{2,3},{3,16},{16,17},{17,18},{18,19},{4,5},{5,6},{6,7}... | collective-permute-start | bytes 6200 | tf_op jit(solution)/shard_map/ppermute | solution.py:23
  335.4 9.0 %collective-permute-start.15 = (f32[2,258,1]{2,1,0:T(8,128)S(1)}, f32[2,258,1]{2,1,0:T(8,128)S(1)}, u32[]{:S(2)}, u32[]{:S(2)}) collective-permute-start(f32[2,258,1]{2,1,0:T(8,128)S(1)} %get-tuple-element.140), channel_id=1, source_target_pairs={{1,0},{2,1},{3,2},{16,3},{17,16},{18,17},{19,18},{5,4},{6,5},{7,6}... | collective-permute-start | bytes 6200 | tf_op jit(solution)/shard_map/ppermute | solution.py:24
  400.1 0.7 copy-start.4
  403.2 0.8 copy-start.7
  420.4 4.2 collective-permute-start.16
  423.2 5.5 collective-permute-start.17
  428.9 8.8 %collective-permute-start.18 = (f32[2,258,1]{2,1,0:T(8,128)S(1)}, f32[2,258,1]{2,1,0:T(8,128)S(1)}, u32[]{:S(2)}, u32[]{:S(2)}) collective-permute-start(f32[2,258,1]{2,1,0:T(8,128)S(1)} %get-tuple-element.137), channel_id=1, source_target_pairs={{0,1},{1,2},{2,3},{3,16},{16,17},{17,18},{18,19},{4,5},{5,6},{6,7}... | collective-permute-start | bytes 6200 | tf_op jit(solution)/shard_map/ppermute | solution.py:23
  432.3 8.8 %collective-permute-start.19 = (f32[2,258,1]{2,1,0:T(8,128)S(1)}, f32[2,258,1]{2,1,0:T(8,128)S(1)}, u32[]{:S(2)}, u32[]{:S(2)}) collective-permute-start(f32[2,258,1]{2,1,0:T(8,128)S(1)} %get-tuple-element.138), channel_id=1, source_target_pairs={{1,0},{2,1},{3,2},{16,3},{17,16},{18,17},{19,18},{5,4},{6,5},{7,6}... | collective-permute-start | bytes 6200 | tf_op jit(solution)/shard_map/ppermute | solution.py:24
  444.9 11.0 %copy-start.5 = (f32[2,2,16384]{2,0,1:T(2,128)S(1)}, f32[2,2,16384]{2,0,1:T(2,128)}, u32[]{:S(2)}) copy-start(f32[2,2,16384]{2,0,1:T(2,128)} %copy-done.4) | copy-start | bytes 786436
  502.6 0.7 copy-start.9
  518.5 4.1 collective-permute-start.20
  521.4 5.5 collective-permute-start.21
  527.0 8.4 %collective-permute-start.22 = (f32[2,258,1]{2,1,0:T(8,128)S(1)}, f32[2,258,1]{2,1,0:T(8,128)S(1)}, u32[]{:S(2)}, u32[]{:S(2)}) collective-permute-start(f32[2,258,1]{2,1,0:T(8,128)S(1)} %get-tuple-element.135), channel_id=1, source_target_pairs={{0,1},{1,2},{2,3},{3,16},{16,17},{17,18},{18,19},{4,5},{5,6},{6,7}... | collective-permute-start | bytes 6200 | tf_op jit(solution)/shard_map/ppermute | solution.py:23
  530.2 9.0 %collective-permute-start.23 = (f32[2,258,1]{2,1,0:T(8,128)S(1)}, f32[2,258,1]{2,1,0:T(8,128)S(1)}, u32[]{:S(2)}, u32[]{:S(2)}) collective-permute-start(f32[2,258,1]{2,1,0:T(8,128)S(1)} %get-tuple-element.136), channel_id=1, source_target_pairs={{1,0},{2,1},{3,2},{16,3},{17,16},{18,17},{19,18},{5,4},{6,5},{7,6}... | collective-permute-start | bytes 6200 | tf_op jit(solution)/shard_map/ppermute | solution.py:24
  543.9 10.8 %copy-start.6 = (f32[2,2,16384]{2,0,1:T(2,128)S(1)}, f32[2,2,16384]{2,0,1:T(2,128)}, u32[]{:S(2)}) copy-start(f32[2,2,16384]{2,0,1:T(2,128)} %copy-done.4) | copy-start | bytes 786436
  543.9 10.8 %all-to-all-start.10 = ((f32[4,2,16384]{2,1,0:T(2,128)}), f32[4,2,16384]{2,1,0:T(2,128)S(1)}, u32[]{:S(2)}, u32[]{:S(2)}) async-start(f32[4,2,16384]{2,1,0:T(2,128)} %copy.150), calls=%async_computation.10 | async-start | bytes 1048576 | tf_op jit(solution)/shard_map/all_to_all | solution.py:188
  548.9 62.0 %copy-start.8 = (f32[2,2,16384]{2,0,1:T(2,128)S(1)}, f32[2,2,16384]{2,0,1:T(2,128)}, u32[]{:S(2)}) copy-start(f32[2,2,16384]{2,0,1:T(2,128)} %copy-done.7) | copy-start | bytes 786436
  548.9 62.0 %copy-start.10 = (f32[2,2,16384]{2,0,1:T(2,128)S(1)}, f32[2,2,16384]{2,0,1:T(2,128)}, u32[]{:S(2)}) copy-start(f32[2,2,16384]{2,0,1:T(2,128)} %copy-done.9) | copy-start | bytes 786436
where the time goes:
time: 636 us; the launch traced here: 628 us
  blocking collectives  334 us (53%)
  waiting for transfers between devices  92.7 us (15%)
  starting transfers between devices  67.7 us (11%)
  local copies, waits for them, and re-layouts  45 us (7%)
  matrix products  33 us (5%)
  other arithmetic  30.3 us (5%)
  between operations  25.3 us (4%)
    psum x4, blocking collectives, shards(): lax.psum((local_products, jnp.sum(images * images)), ('chip', 'row', 'grp'))  155 us
    psum x2, blocking collectives, shards(): lax.psum(jnp.sum(residual * residual), ('chip', 'row', 'grp'))  77.2 us
    all_to_all x6, blocking collectives, to_tiles(): lax.all_to_all(select(receive_matrix.T, vector), 'row', split_axis=0, con...  68.4 us
    ppermute x12, waiting for transfers between devices, extended(): after = lax.ppermute(initial, axis, down)  46.7 us
    ppermute x12, starting transfers between devices, extended(): before = lax.ppermute(last, axis, up)  39.2 us
    all_to_all x3, blocking collectives, apply_system(): lax.all_to_all(select(send_matrix, images), 'row', split_axis=0, concat_a...  32.8 us
    dot_general x24, matrix products, select(): jnp.einsum('st,tcx->scx', matrix, blocks, precision=lax.Precision.HIGHEST)  32.8 us
    ppermute x12, waiting for transfers between devices, extended(): before = lax.ppermute(last, axis, up)  21.9 us
  transfers between devices with their start and end apart: 27, of which 21 were waited for; matrix products, arithmetic and copies ran while one was open for 1% of the time, Pallas kernels for 0%

commit v1 on v0

v1 whole, which is shorter than its diff:
```python
import functools

import jax
import jax.numpy as jnp
from jax import lax
from jax.experimental import pallas as pl
from jax.experimental.pallas import tpu as pltpu
from jax.sharding import PartitionSpec as P

MESH = pl.DeviceIdType.MESH
BS = 128
DMIN_SQ = 0.25
STEPS = 4
VEL = STEPS
ROWS_P = 32
ROWS_S = 16
PAD = 8
DIRS = ((-1, 0), (1, 0), (0, 1), (1, 1), (-1, 1), (0, -1), (1, -1), (-1, -1))
PAIRS = [(i, j) for j in range(STEPS + 1) for i in range(j + 1)]
INDEX = {pair: n for n, pair in enumerate(PAIRS)}
COUNT = 16


def neighbour_sum(p, p_n, p_s, q, q_n, q_s):
    tq = q_s - q_n
    tp = p_s - p_n
    p5 = p
    q5 = 5.0 * q
    return (5.0 * (p_n + p_s), p5 + tq, p5 - tq), (q_n + q_s, q5 + tp, q5 - tp)


def scalars(gram):
    n = STEPS + 1

    def g(i, j):
        return gram[INDEX[(min(i, j), max(i, j))]]

    def dot(x, y):
        total = None
        for j in range(n):
            if y[j] is None:
                continue
            inner = None
            for i in range(n):
                if x[i] is None:
                    continue
                term = x[i] * g(i, j)
                inner = term if inner is None else inner + term
            term = inner * y[j]
            total = term if total is None else total + term
        return total

    def shift(x):
        return [None] + x[: n - 1]

    def add(x, y):
        return [b if a is None else a if b is None else a + b for a, b in zip(x, y)]

    def cycle(r):
        w1 = add(r, shift(r))
        w2 = shift(w1)
        b1, b2 = dot(r, w1), dot(r, w2)
        g11, g12, g22 = dot(w1, w1), dot(w1, w2), dot(w2, w2)
        det = g11 * g22 - g12 * g12
        good = det > 0.0
        inv = 1.0 / jnp.where(good, det, 1.0)
        single = jnp.where(g11 > 0.0, b1 / jnp.where(g11 > 0.0, g11, 1.0), 0.0)
        a = jnp.where(good, (b1 * g22 - b2 * g12) * inv, single)
        b = jnp.where(good, (g11 * b2 - g12 * b1) * inv, 0.0)
        return a, b

    one = jnp.ones_like(gram[0])
    a0, b0 = cycle([one, None, None, None, None])
    c = [1.0 - a0, -(a0 + b0), -b0]
    a1, b1 = cycle(c + [None, None])
    return (
        a0 + a1 * c[0],
        b0 + a1 * c[1] + b1 * c[0],
        a1 * c[2] + b1 * c[1],
        b1 * c[2],
    )


def kernel(
    sizes,
    vel_ref,
    stress_ref,
    mass_ref,
    drag_ref,
    strength_ref,
    ice_ref,
    ocean_ref,
    listed_ref,
    out_ref,
    D,
    V,
    Z0,
    Z1,
    CO,
    EB,
    RB,
    HC,
    GB,
    GX,
    R1,
    R2,
    send_sem,
    recv_sem,
    s1,
    r1,
    s2,
    r2,
):
    n_chip, n_row, n_grp, rows, cols = sizes
    n_col = n_chip * n_grp
    nbi, nbj = rows // BS, cols // BS
    chip = lax.axis_index("chip")
    row = lax.axis_index("row")
    grp = lax.axis_index("grp")
    col = chip * n_grp + grp

    def device(dr, dc):
        r = lax.rem(row + (dr + n_row), n_row)
        c = lax.rem(col + (dc + n_col), n_col)
        return (lax.div(c, n_grp), r, lax.rem(c, n_grp))

    partners = list(DIRS)
    for o in range(1, n_row):
        if o not in (1, n_row - 1):
            partners.append((o, 0))
    for o in range(1, n_col):
        if o not in (1, n_col - 1):
            partners.append((0, o))
    barrier = pltpu.get_barrier_semaphore()
    for dr, dc in partners:
        pl.semaphore_signal(barrier, inc=1, device_id=device(dr, dc), device_id_type=MESH)

    has_n = row > 0
    has_s = row < n_row - 1
    has_w = col > 0
    has_e = col < n_col - 1

    lane_p = lax.broadcasted_iota(jnp.int32, (ROWS_P, BS), 1)
    lane_s = lax.broadcasted_iota(jnp.int32, (ROWS_S, BS), 1)
    sub_s = lax.broadcasted_iota(jnp.int32, (ROWS_S, BS), 0)
    eye = lax.broadcasted_iota(jnp.int32, (BS, BS), 0) == lax.broadcasted_iota(jnp.int32, (BS, BS), 1)
    lane_1 = lax.broadcasted_iota(jnp.int32, (1, BS), 1)

    def east(x):
        return pltpu.roll(x, BS - 1, 1)

    def west(x):
        return pltpu.roll(x, 1, 1)

    def copies(slot, dirs):
        found = []
        for d in dirs:
            dr, dc = DIRS[d]
            if dc == 0:
                first, there = (PAD, PAD + rows) if dr < 0 else (rows, 0)
                src = D.at[slot, :, :, pl.ds(first, PAD), :]
                dst = D.at[slot, :, :, pl.ds(there, PAD), :]
            else:
                src = EB.at[slot, 0 if dc > 0 else 1]
                dst = RB.at[slot, d - 2]
            found.append(
                pltpu.make_async_remote_copy(
                    src_ref=src,
                    dst_ref=dst,
                    send_sem=send_sem.at[slot, d],
                    recv_sem=recv_sem.at[slot, d],
                    device_id=device(dr, dc),
                    device_id_type=MESH,
                )
            )
        return found

    def send_halo(slot, dirs):
        for side in range(2):
            bj, lane = (nbj - 1, BS - 1) if side == 0 else (0, 0)
            lines = []
            for comp in range(2):
                for bi in range(nbi):
                    x = D[slot, comp, bj, pl.ds(PAD + bi * BS, BS), :]
                    edge = jnp.broadcast_to(x[:, lane : lane + 1], (BS, BS))
                    lines.append(jnp.sum(jnp.where(eye, edge, 0.0), axis=0, keepdims=True))
            lines.append(jnp.zeros((8 - 2 * nbi, BS), jnp.float32))
            EB[slot, side] = jnp.concatenate(lines, axis=0)
        moved = copies(slot, dirs)
        for copy in moved:
            copy.start()
        return moved

    def take_halo(slot, moved, with_corners):
        for copy in moved:
            copy.wait_recv()
        for comp in range(2):
            for bj in range(nbj):
                top = D[slot, comp, bj, 0:PAD, :]
                D[slot, comp, bj, 0:PAD, :] = jnp.where(has_n, top, 0.0)
                low = D[slot, comp, bj, PAD + rows : PAD + rows + PAD, :]
                D[slot, comp, bj, PAD + rows : PAD + rows + PAD, :] = jnp.where(has_s, low, 0.0)
        for side in range(2):
            present = has_w if side == 0 else has_e
            block = RB[slot, 3 * side]
            lines = [[block[c * nbi + b : c * nbi + b + 1] for b in range(nbi)] for c in range(2)]
            if not with_corners:
                for c in range(2):
                    for b in range(nbi):
                        HC[side, c * nbi + b : c * nbi + b + 1, :] = jnp.where(present, lines[c][b], 0.0)
                continue
            above = RB[slot, 3 * side + 1]
            below = RB[slot, 3 * side + 2]
            steps = []
            for c in range(2):
                line = []
                for b in range(nbi):
                    up = west(lines[c][b - 1]) if b > 0 else jnp.where(has_n, west(above[c * nbi + nbi - 1 : c * nbi + nbi]), 0.0)
                    down = east(lines[c][b + 1]) if b < nbi - 1 else jnp.where(has_s, east(below[c * nbi : c * nbi + 1]), 0.0)
                    north = jnp.where(lane_1 == 0, up, west(lines[c][b]))
                    south = jnp.where(lane_1 == BS - 1, down, east(lines[c][b]))
                    line.append(south - north)
                steps.append(line)
            sign = -1.0 if side == 0 else 1.0
            for b in range(nbi):
                HC[side, b : b + 1, :] = jnp.where(present, lines[0][b] + sign * steps[1][b], 0.0)
                HC[side, nbi + b : nbi + b + 1, :] = jnp.where(present, 5.0 * lines[1][b] + sign * steps[0][b], 0.0)

    def halo_column(side, comp, bi, r0):
        line = HC[side, pl.ds(comp * nbi + bi, 1), :]
        kept = jnp.where(lane_s == sub_s + r0, jnp.broadcast_to(line, (ROWS_S, BS)), 0.0)
        return jnp.sum(kept, axis=1, keepdims=True)

    def fold(x):
        total = x[0:8]
        for n in range(1, ROWS_S // 8):
            total = total + x[8 * n : 8 * n + 8]
        return total

    for comp in range(2):
        for bj in range(nbj):
            D[VEL, comp, bj, PAD : PAD + rows, :] = vel_ref[comp, :, bj * BS : (bj + 1) * BS]
    pl.semaphore_wait(barrier, len(partners))
    vel_dirs = (0, 1, 2, 5)
    pending = [send_halo(VEL, vel_dirs)]
    for Z in (Z0, Z1):
        for comp in range(2):
            for b in range(nbi * nbj):
                Z[comp, b, 0:PAD, :] = jnp.zeros((PAD, BS), jnp.float32)
                Z[comp, b, PAD + BS : PAD + BS + PAD, :] = jnp.zeros((PAD, BS), jnp.float32)
    live = []
    for b in range(nbi * nbj):
        wanted = row * (nbi * nbj) + b
        flag = jnp.float32(0.0)
        for n in range(listed_ref.shape[1]):
            flag = jnp.maximum(flag, jnp.where(listed_ref[0, n] == wanted, 1.0, 0.0))
        live.append(flag)
    take_halo(VEL, pending[0], False)

    per_block = BS // ROWS_S
    zero8 = jnp.zeros((8, BS), jnp.float32)

    def setup(t, acc):
        bi = lax.div(t, per_block)
        r0 = lax.rem(t, per_block) * ROWS_S
        start = pl.multiple_of(t * ROWS_S, ROWS_S)
        here = pl.ds(start, ROWS_S)
        us, vs = [], []
        for bj in range(nbj):
            us.append([D[VEL, 0, bj, pl.ds(PAD + start + d, ROWS_S), :] for d in (-1, 0, 1)])
            vs.append([D[VEL, 1, bj, pl.ds(PAD + start + d, ROWS_S), :] for d in (-1, 0, 1)])

        def across(parts, comp):
            e = [east(x[1]) for x in parts]
            w = [west(x[1]) for x in parts]
            edge_e, edge_w = halo_column(1, comp, bi, r0), halo_column(0, comp, bi, r0)
            found = []
            for bj in range(nbj):
                right = e[bj + 1] if bj < nbj - 1 else edge_e
                left = w[bj - 1] if bj > 0 else edge_w
                found.append(jnp.where(lane_s == BS - 1, right, e[bj]) - jnp.where(lane_s == 0, left, w[bj]))
            return found

        du, dv = across(us, 0), across(vs, 1)
        for bj in range(nbj):
            lanes = slice(bj * BS, (bj + 1) * BS)
            e11 = 0.5 * (us[bj][2] - us[bj][0])
            e22 = 0.5 * dv[bj]
            e12 = 0.25 * (du[bj] + vs[bj][2] - vs[bj][0])
            deform = 1.25 * (e11 * e11 + e22 * e22) + e12 * e12 + 1.5 * e11 * e22
            ocean = ocean_ref[here, lanes].astype(jnp.float32)
            ice = ice_ref[here, lanes].astype(jnp.float32)
            mass = mass_ref[here, lanes]
            zeta = ocean * ice * strength_ref[here, lanes] / (2.0 * jnp.sqrt(deform + DMIN_SQ))
            total = ocean * (mass + drag_ref[here, lanes]) + (1.0 - ocean) + 3.0 * zeta
            inv = 1.0 / total
            flag = live[bj]
            for b in range(1, nbi):
                flag = jnp.where(bi == b, live[b * nbj + bj], flag)
            scaled = ocean * flag
            CO[0, bj, here, :] = inv
            CO[1, bj, here, :] = 0.2 * zeta * inv
            CO[2, bj, here, :] = flag * total
            CO[3, bj, here, :] = flag * (0.25 * zeta)
            for comp in range(2):
                vel = us[bj][1] if comp == 0 else vs[bj][1]
                rhs = scaled * (stress_ref[comp, here, lanes] + mass * vel)
                V[0, comp, bj, here, :] = rhs
                Z0[comp, bi * nbj + bj, pl.ds(PAD + r0, ROWS_S), :] = rhs * inv
                acc = acc + fold(rhs * rhs)
        return acc

    def put_products(step, values):
        for i, value in enumerate(values):
            n = INDEX[(i, step)]
            GB[n : n + 1, :] = jnp.sum(value, axis=0, keepdims=True)

    GB[COUNT - 1 : COUNT, :] = jnp.zeros((1, BS), jnp.float32)
    put_products(0, [lax.fori_loop(0, rows // ROWS_S, setup, zero8)])

    def block_sums(Z, b, c):
        first = PAD + c * ROWS_P
        p = [Z[0, b, pl.ds(first + d, ROWS_P), :] for d in (-1, 0, 1)]
        q = [Z[1, b, pl.ds(first + d, ROWS_P), :] for d in (-1, 0, 1)]
        sums = []
        for base, ye, yw in neighbour_sum(p[1], p[0], p[2], q[1], q[0], q[2]):
            e = jnp.where(lane_p == BS - 1, 0.0, east(ye))
            w = jnp.where(lane_p == 0, 0.0, west(yw))
            sums.append(base + e + w)
        return (p[1], q[1]), sums

    def sweep(slot):
        def first(b, carry):
            bi, bj = lax.div(b, nbj), lax.rem(b, nbj)
            for c in range(BS // ROWS_P):
                z, sums = block_sums(Z0, b, c)
                k = CO[1, bj, pl.ds(pl.multiple_of(bi * BS, BS) + c * ROWS_P, ROWS_P), :]
                for comp in range(2):
                    Z1[comp, b, PAD + c * ROWS_P : PAD + (c + 1) * ROWS_P, :] = z[comp] + k * sums[comp]
            return carry

        def second(b, carry):
            bi, bj = lax.div(b, nbj), lax.rem(b, nbj)
            for c in range(BS // ROWS_P):
                z, sums = block_sums(Z1, b, c)
                at = pl.multiple_of(bi * BS, BS) + c * ROWS_P
                k = CO[1, bj, pl.ds(at, ROWS_P), :]
                for comp in range(2):
                    z0 = Z0[comp, b, PAD + c * ROWS_P : PAD + (c + 1) * ROWS_P, :]
                    D[slot, comp, bj, pl.ds(PAD + at, ROWS_P), :] = 0.2 * z[comp] + 0.8 * z0 + k * sums[comp]
            return carry

        lax.fori_loop(0, nbi * nbj, first, 0)
        lax.fori_loop(0, nbi * nbj, second, 0)

    def operator(step):
        last = step == STEPS - 1

        def body(t, acc):
            acc = list(acc)
            bi = lax.div(t, per_block)
            r0 = lax.rem(t, per_block) * ROWS_S
            start = pl.multiple_of(t * ROWS_S, ROWS_S)
            here = pl.ds(start, ROWS_S)
            z, base, es, ws = [], [], [[], []], [[], []]
            for bj in range(nbj):
                p = [D[step, 0, bj, pl.ds(PAD + start + d, ROWS_S), :] for d in (-1, 0, 1)]
                q = [D[step, 1, bj, pl.ds(PAD + start + d, ROWS_S), :] for d in (-1, 0, 1)]
                parts = neighbour_sum(p[1], p[0], p[2], q[1], q[0], q[2])
                z.append((p[1], q[1]))
                base.append([part[0] for part in parts])
                for comp in range(2):
                    es[comp].append(east(parts[comp][1]))
                    ws[comp].append(west(parts[comp][2]))
            for comp in range(2):
                edge_e, edge_w = halo_column(1, comp, bi, r0), halo_column(0, comp, bi, r0)
                for bj in range(nbj):
                    right = es[comp][bj + 1] if bj < nbj - 1 else edge_e
                    left = ws[comp][bj - 1] if bj > 0 else edge_w
                    e = jnp.where(lane_s == BS - 1, right, es[comp][bj])
                    w = jnp.where(lane_s == 0, left, ws[comp][bj])
                    image = CO[2, bj, here, :] * z[bj][comp] - CO[3, bj, here, :] * (base[bj][comp] + e + w)
                    old = V[step, comp, bj, here, :]
                    new = image - old
                    if not last:
                        V[step + 1, comp, bj, here, :] = new
                        Z0[comp, bi * nbj + bj, pl.ds(PAD + r0, ROWS_S), :] = new * CO[0, bj, here, :]
                    for i in range(step + 1):
                        earlier = old if i == step else V[i, comp, bj, here, :]
                        acc[i] = acc[i] + fold(new * earlier)
                    acc[step + 1] = acc[step + 1] + fold(new * new)
            return tuple(acc)

        put_products(step + 1, lax.fori_loop(0, rows // ROWS_S, body, (zero8,) * (step + 2)))

    for step in range(STEPS):
        sweep(step)
        pending.append(send_halo(step, range(len(DIRS))))
        take_halo(step, pending[-1], True)
        operator(step)

    def spread(src, buffer, count, send, recv, along_row):
        moved = [
            pltpu.make_async_remote_copy(
                src_ref=src,
                dst_ref=buffer.at[o - 1],
                send_sem=send.at[o - 1],
                recv_sem=recv.at[o - 1],
                device_id=device(o, 0) if along_row else device(0, o),
                device_id_type=MESH,
            )
            for o in range(1, count)
        ]
        for copy in moved:
            copy.start()
        for copy in moved:
            copy.wait_recv()
        pending.append(moved)
        total = src[...]
        for o in range(1, count):
            total = total + buffer[o - 1]
        return total

    GX[...] = spread(GB, R1, n_row, s1, r1, True)
    products = jnp.sum(spread(GX, R2, n_col, s2, r2, False), axis=1, keepdims=True)
    weights = scalars([products[n : n + 1] for n in range(len(PAIRS))])

    for comp in range(2):
        for bj in range(nbj):
            total = None
            for step in range(STEPS):
                term = weights[step] * D[step, comp, bj, PAD : PAD + rows, :]
                total = term if total is None else total + term
            out_ref[comp, :, bj * BS : (bj + 1) * BS] = total
    for moved in pending:
        for copy in moved:
            copy.wait_send()


def solution(mesh):
    n_chip, n_row, n_grp = mesh.shape["chip"], mesh.shape["row"], mesh.shape["grp"]

    def shards(old_velocity, surface_stress, mass_term, ocean_drag, strength, ice_mask, ocean_mask, ice_blocks):
        _, rows, cols = old_velocity.shape
        nbi, nbj = rows // BS, cols // BS
        vmem = pl.BlockSpec(memory_space=pltpu.VMEM)
        f32 = jnp.float32
        n_col = n_chip * n_grp
        dma = pltpu.SemaphoreType.DMA
        return pl.pallas_call(
            functools.partial(kernel, (n_chip, n_row, n_grp, rows, cols)),
            out_shape=jax.ShapeDtypeStruct(old_velocity.shape, f32),
            in_specs=[vmem] * 7 + [pl.BlockSpec(memory_space=pltpu.SMEM)],
            out_specs=vmem,
            scratch_shapes=[
                pltpu.VMEM((STEPS + 1, 2, nbj, rows + 2 * PAD, BS), f32),
                pltpu.VMEM((STEPS, 2, nbj, rows, BS), f32),
                pltpu.VMEM((2, nbi * nbj, BS + 2 * PAD, BS), f32),
                pltpu.VMEM((2, nbi * nbj, BS + 2 * PAD, BS), f32),
                pltpu.VMEM((4, nbj, rows, BS), f32),
                pltpu.VMEM((STEPS + 1, 2, 8, BS), f32),
                pltpu.VMEM((STEPS + 1, 6, 8, BS), f32),
                pltpu.VMEM((2, 8, BS), f32),
                pltpu.VMEM((COUNT, BS), f32),
                pltpu.VMEM((COUNT, BS), f32),
                pltpu.VMEM((n_row - 1, COUNT, BS), f32),
                pltpu.VMEM((n_col - 1, COUNT, BS), f32),
                dma((STEPS + 1, len(DIRS))),
                dma((STEPS + 1, len(DIRS))),
                dma((n_row - 1,)),
                dma((n_row - 1,)),
                dma((n_col - 1,)),
                dma((n_col - 1,)),
            ],
            compiler_params=pltpu.CompilerParams(
                collective_id=0, has_side_effects=True, vmem_limit_bytes=40 * 1024 * 1024
            ),
        )(old_velocity, surface_stress, mass_term, ocean_drag, strength, ice_mask, ocean_mask, ice_blocks)

    return jax.shard_map(
        shards,
        mesh=mesh,
        in_specs=(
            P(None, "row", ("chip", "grp")),
            P(None, "row", ("chip", "grp")),
            P("row", ("chip", "grp")),
            P("row", ("chip", "grp")),
            P("row", ("chip", "grp")),
            P("row", ("chip", "grp")),
            P("row", ("chip", "grp")),
            P(("chip", "grp"), None),
        ),
        out_specs=P(None, "row", ("chip", "grp")),
        check_vma=False,
    )
```

time: 636 us -> 58.8 us (0.09); the launches traced: 628 us -> 58.4 us
  blocking collectives: 334 us -> 0 us
  waiting for transfers between devices: 92.7 us -> 0 us
  starting transfers between devices: 67.7 us -> 0 us
  Pallas kernels: 0 us -> 50.1 us
  local copies, waits for them, and re-layouts: 45 us -> 8.28 us
  matrix products: 33 us -> 0 us
  other arithmetic: 30.3 us -> 0 us
  between operations: 25.3 us -> 0.02 us
    psum x6 -> x0, blocking collectives: 232 us -> none  [the longest x4 155 us: shards(): lax.psum((local_products, jnp.sum(images * images)), ('chip', 'row', 'grp'))]
    all_to_all x9 -> x0, blocking collectives: 101 us -> none  [the longest x6 68.4 us: to_tiles(): lax.all_to_all(select(receive_matrix.T, vector), 'row', split_axis=0, con...]
    ppermute x24 -> x0, waiting for transfers between devices: 68.6 us -> none  [the longest x12 46.7 us: extended(): after = lax.ppermute(initial, axis, down)]
    ppermute x24 -> x0, starting transfers between devices: 55.3 us -> none  [the longest x12 39.2 us: extended(): before = lax.ppermute(last, axis, up)]
    pallas_call x0 -> x1, Pallas kernels: none -> 50.1 us  [shards(): pl.pallas_call(functools.partial(kernel, (n_chip, n_row, n_grp, rows, col...]
    dot_general x25 -> x0, matrix products: 33 us -> none  [the longest x24 32.8 us: select(): jnp.einsum('st,tcx->scx', matrix, blocks, precision=lax.Precision.HIGHEST)]
    all_to_all x3 -> x0, waiting for transfers between devices: 24.1 us -> none  [the longest x1 13.7 us: shards(): lax.all_to_all(outgoing, 'row', split_axis=0, concat_axis=0, tiled=True)]
    all_to_all x3 -> x0, starting transfers between devices: 12.4 us -> none  [the longest x2 7.79 us: apply_system(): lax.all_to_all(select(send_matrix, images), 'row', split_axis=0, concat_a...]
  transfers between devices with their start and end apart: 27 -> 0, of which waited for: 21 -> 0; matrix products, arithmetic and copies ran while one was open for 1% -> 0% of each run, Pallas kernels for 0% -> 0%
where the time goes in v1:
time: 58.8 us; the launch traced here: 58.4 us
  Pallas kernels  50.1 us (85%)
  local copies, waits for them, and re-layouts  8.28 us (14%)
    pallas_call x1, Pallas kernels, shards(): pl.pallas_call(functools.partial(kernel, (n_chip, n_row, n_grp, rows, col...  50.1 us
    unnamed x17, local copies, waits for them, and re-layouts  8.28 us

profile of v1, /device:TPU:0, one launch (start us, length us, event | category | flops | bytes accessed | tf_op | source)
XLA Modules:
  0.0 58.4 jit_solution(4041774822948115380)
XLA Ops:
  0.0 0.0 copy-start
  0.0 1.0 %copy-done = f32[2,256,256]{2,1,0:T(8,128)S(1)} copy-done((f32[2,256,256]{2,1,0:T(8,128)S(1)}, f32[2,256,256]{2,1,0:T(8,128)}, u32[]{:S(2)}) %copy-start) | copy-done | bytes 524312
  1.0 0.0 copy-start.1
  1.0 1.0 %copy-done.1 = f32[2,256,256]{2,1,0:T(8,128)S(1)} copy-done((f32[2,256,256]{2,1,0:T(8,128)S(1)}, f32[2,256,256]{2,1,0:T(8,128)}, u32[]{:S(2)}) %copy-start.1) | copy-done | bytes 524312
  2.1 0.0 copy-start.2
  2.1 0.9 %copy-done.2 = f32[256,256]{1,0:T(8,128)S(1)} copy-done((f32[256,256]{1,0:T(8,128)S(1)}, f32[256,256]{1,0:T(8,128)}, u32[]{:S(2)}) %copy-start.2) | copy-done | bytes 262168
  3.0 0.0 copy-start.3
  3.0 0.9 %copy-done.3 = f32[256,256]{1,0:T(8,128)S(1)} copy-done((f32[256,256]{1,0:T(8,128)S(1)}, f32[256,256]{1,0:T(8,128)}, u32[]{:S(2)}) %copy-start.3) | copy-done | bytes 262168
  4.0 0.0 copy-start.4
  4.0 0.9 %copy-done.4 = f32[256,256]{1,0:T(8,128)S(1)} copy-done((f32[256,256]{1,0:T(8,128)S(1)}, f32[256,256]{1,0:T(8,128)}, u32[]{:S(2)}) %copy-start.4) | copy-done | bytes 262168
  4.9 0.0 copy-start.5
  4.9 0.9 %copy-done.5 = s32[256,256]{1,0:T(8,128)S(1)} copy-done((s32[256,256]{1,0:T(8,128)S(1)}, s32[256,256]{1,0:T(8,128)}, u32[]{:S(2)}) %copy-start.5) | copy-done | bytes 262168
  5.9 0.0 copy-start.6
  5.9 0.9 %copy-done.6 = s32[256,256]{1,0:T(8,128)S(1)} copy-done((s32[256,256]{1,0:T(8,128)S(1)}, s32[256,256]{1,0:T(8,128)}, u32[]{:S(2)}) %copy-start.6) | copy-done | bytes 262168
  6.8 0.0 copy-start.7
  6.8 0.7 %copy-done.7 = s32[1,8]{1,0:T(1,128)S(1)} copy-done((s32[1,8]{1,0:T(1,128)S(1)}, s32[1,8]{1,0:T(1,128)}, u32[]{:S(2)}) %copy-start.7) | copy-done | bytes 56
  7.5 50.1 %shard_map.82 = f32[2,256,256]{2,1,0:T(8,128)S(1)} custom-call(f32[2,256,256]{2,1,0:T(8,128)S(1)} %copy-done, f32[2,256,256]{2,1,0:T(8,128)S(1)} %copy-done.1, f32[256,256]{1,0:T(8,128)S(1)} %copy-done.2, f32[256,256]{1,0:T(8,128)S(1)} %copy-done.3, f32[256,256]{1,0:T(8,128)S(1)} %copy-done.4, s32[256,256]{1,0:T(8,128)S(1)} %copy-done.5, ...), custom_call_target="tpu_custom_call" | custom-call | tf_op jit(solution)/shard_map/pallas_call | solution.py:450
  57.6 0.8 %copy.10 = f32[2,256,256]{2,1,0:T(8,128)} copy(f32[2,256,256]{2,1,0:T(8,128)S(1)} %shard_map.82) | data formatting | bytes 1048576
Async XLA Ops:
  0.0 1.0 %copy-start = (f32[2,256,256]{2,1,0:T(8,128)S(1)}, f32[2,256,256]{2,1,0:T(8,128)}, u32[]{:S(2)}) copy-start(f32[2,256,256]{2,1,0:T(8,128)} %vel_ref.1) | copy-start | bytes 1572868
  1.0 1.0 %copy-start.1 = (f32[2,256,256]{2,1,0:T(8,128)S(1)}, f32[2,256,256]{2,1,0:T(8,128)}, u32[]{:S(2)}) copy-start(f32[2,256,256]{2,1,0:T(8,128)} %stress_ref.1) | copy-start | bytes 1572868
  2.1 0.9 %copy-start.2 = (f32[256,256]{1,0:T(8,128)S(1)}, f32[256,256]{1,0:T(8,128)}, u32[]{:S(2)}) copy-start(f32[256,256]{1,0:T(8,128)} %mass_ref.1) | copy-start | bytes 786436
  3.0 0.9 %copy-start.3 = (f32[256,256]{1,0:T(8,128)S(1)}, f32[256,256]{1,0:T(8,128)}, u32[]{:S(2)}) copy-start(f32[256,256]{1,0:T(8,128)} %drag_ref.1) | copy-start | bytes 786436
  4.0 0.9 %copy-start.4 = (f32[256,256]{1,0:T(8,128)S(1)}, f32[256,256]{1,0:T(8,128)}, u32[]{:S(2)}) copy-start(f32[256,256]{1,0:T(8,128)} %strength_ref.1) | copy-start | bytes 786436
  4.9 0.9 %copy-start.5 = (s32[256,256]{1,0:T(8,128)S(1)}, s32[256,256]{1,0:T(8,128)}, u32[]{:S(2)}) copy-start(s32[256,256]{1,0:T(8,128)} %ice_ref.1) | copy-start | bytes 786436
  5.9 0.9 %copy-start.6 = (s32[256,256]{1,0:T(8,128)S(1)}, s32[256,256]{1,0:T(8,128)}, u32[]{:S(2)}) copy-start(s32[256,256]{1,0:T(8,128)} %ocean_ref.1) | copy-start | bytes 786436
  6.8 0.7 %copy-start.7 = (s32[1,8]{1,0:T(1,128)S(1)}, s32[1,8]{1,0:T(1,128)}, u32[]{:S(2)}) copy-start(s32[1,8]{1,0:T(1,128)} %listed_ref.1) | copy-start | bytes 100

commit v2 on v1

v2 whole, which is shorter than its diff:
```python
import functools

import jax
import jax.numpy as jnp
from jax import lax
from jax.experimental import pallas as pl
from jax.experimental.pallas import tpu as pltpu
from jax.sharding import PartitionSpec as P

MESH = pl.DeviceIdType.MESH
BS = 128
DMIN_SQ = 0.25
STEPS = 4
DEPTH = 16
PAD = 8
ROWS = 16
PACKED = BS // DEPTH
FIELDS = 6
DIAG = 4
DIRS = ((-1, 0), (1, 0), (0, 1), (1, 1), (-1, 1), (0, -1), (1, -1), (-1, -1))
PAIRS = [(i, j) for j in range(STEPS + 1) for i in range(j + 1)]
INDEX = {pair: n for n, pair in enumerate(PAIRS)}
COUNT = 16


def neighbour_sum(p, p_n, p_s, q, q_n, q_s):
    tq = q_s - q_n
    tp = p_s - p_n
    q5 = 5.0 * q
    return (5.0 * (p_n + p_s), p + tq, p - tq), (q_n + q_s, q5 + tp, q5 - tp)


def scalars(gram):
    n = STEPS + 1

    def g(i, j):
        return gram[INDEX[(min(i, j), max(i, j))]]

    def dot(x, y):
        total = None
        for j in range(n):
            if y[j] is None:
                continue
            inner = None
            for i in range(n):
                if x[i] is None:
                    continue
                term = x[i] * g(i, j)
                inner = term if inner is None else inner + term
            term = inner * y[j]
            total = term if total is None else total + term
        return total

    def shift(x):
        return [None] + x[: n - 1]

    def add(x, y):
        return [b if a is None else a if b is None else a + b for a, b in zip(x, y)]

    def cycle(r):
        w1 = add(r, shift(r))
        w2 = shift(w1)
        b1, b2 = dot(r, w1), dot(r, w2)
        g11, g12, g22 = dot(w1, w1), dot(w1, w2), dot(w2, w2)
        det = g11 * g22 - g12 * g12
        good = det > 0.0
        inv = 1.0 / jnp.where(good, det, 1.0)
        single = jnp.where(g11 > 0.0, b1 / jnp.where(g11 > 0.0, g11, 1.0), 0.0)
        a = jnp.where(good, (b1 * g22 - b2 * g12) * inv, single)
        b = jnp.where(good, (g11 * b2 - g12 * b1) * inv, 0.0)
        return a, b

    one = jnp.ones_like(gram[0])
    a0, b0 = cycle([one, None, None, None, None])
    c = [1.0 - a0, -(a0 + b0), -b0]
    a1, b1 = cycle(c + [None, None])
    return (
        a0 + a1 * c[0],
        b0 + a1 * c[1] + b1 * c[0],
        a1 * c[2] + b1 * c[1],
        b1 * c[2],
    )


def kernel(
    sizes,
    vel_hbm,
    stress_hbm,
    mass_hbm,
    drag_hbm,
    strength_hbm,
    ice_hbm,
    ocean_hbm,
    listed_ref,
    out_ref,
    vel_ref,
    stress_ref,
    mass_ref,
    drag_ref,
    strength_ref,
    ice_ref,
    ocean_ref,
    X,
    D,
    V,
    Z0,
    Z1,
    CO,
    PB,
    PR,
    CB,
    CR,
    GB,
    GX,
    R1,
    R2,
    load_sem,
    send_sem,
    recv_sem,
    s1,
    r1,
    s2,
    r2,
):
    n_chip, n_row, n_grp, rows, cols = sizes
    n_col = n_chip * n_grp
    nbi, nbj = rows // BS, cols // BS
    nl = nbj + 1
    group = rows // PACKED
    chunks = (rows + 2 * DEPTH) // ROWS
    per_block = BS // ROWS
    chip = lax.axis_index("chip")
    row = lax.axis_index("row")
    grp = lax.axis_index("grp")
    col = chip * n_grp + grp

    loads = [
        pltpu.make_async_copy(src, dst, load_sem.at[n])
        for n, (src, dst) in enumerate(
            (
                (vel_hbm, vel_ref),
                (mass_hbm, mass_ref),
                (ocean_hbm, ocean_ref),
                (stress_hbm, stress_ref),
                (drag_hbm, drag_ref),
                (strength_hbm, strength_ref),
                (ice_hbm, ice_ref),
            )
        )
    ]
    for load in loads:
        load.start()

    def device(dr, dc):
        r = lax.rem(row + (dr + n_row), n_row)
        c = lax.rem(col + (dc + n_col), n_col)
        return (lax.div(c, n_grp), r, lax.rem(c, n_grp))

    partners = list(DIRS)
    for o in range(2, n_row - 1):
        partners.append((o, 0))
    for o in range(2, n_col - 1):
        partners.append((0, o))
    barrier = pltpu.get_barrier_semaphore()
    for dr, dc in partners:
        pl.semaphore_signal(barrier, inc=1, device_id=device(dr, dc), device_id_type=MESH)

    has_n = row > 0
    has_s = row < n_row - 1
    has_w = col > 0
    has_e = col < n_col - 1

    def exists(dr, dc):
        found = None
        for offset, low, high in ((dr, has_n, has_s), (dc, has_w, has_e)):
            if offset:
                flag = low if offset < 0 else high
                found = flag if found is None else jnp.logical_and(found, flag)
        return found

    lane = lax.broadcasted_iota(jnp.int32, (ROWS, BS), 1)
    lane_g = lax.broadcasted_iota(jnp.int32, (group, BS), 1)
    first_lane, last_lane = lane == 0, lane == BS - 1

    def east(x):
        return pltpu.roll(x, BS - 1, 1)

    def west(x):
        return pltpu.roll(x, 1, 1)

    def turn(x, amount):
        amount = amount % BS
        return x if amount == 0 else pltpu.roll(x, amount, 1)

    def filling(field):
        return 1.0 if field == DIAG else 0.0

    zero8 = jnp.zeros((PAD, BS), jnp.float32)
    edges = [0, PAD + DEPTH]
    for b in range(nbi):
        edges.append(edges[-1] + PAD + BS)
    edges.append(edges[-1] + PAD + DEPTH)
    for j in range(nl):
        for comp in range(2):
            for at in edges:
                Z0[comp, j, at : at + PAD, :] = zero8
                Z1[comp, j, at : at + PAD, :] = zero8
            for at in (0, PAD + rows + 2 * DEPTH):
                X[comp, j, at : at + PAD, :] = zero8
                for step in range(STEPS):
                    D[step, comp, j, at : at + PAD, :] = zero8

    live = []
    for b in range(nbi * nbj):
        wanted = row * (nbi * nbj) + b
        flag = jnp.float32(0.0)
        for n in range(listed_ref.shape[1]):
            flag = jnp.maximum(flag, jnp.where(listed_ref[0, n] == wanted, 1.0, 0.0))
        live.append(flag)

    for load in loads:
        load.wait()

    def local(t, carry):
        bi = lax.div(t, per_block)
        start = pl.multiple_of(t * ROWS, ROWS)
        here = pl.ds(start, ROWS)
        there = pl.ds(pl.multiple_of(PAD + DEPTH + start, PAD), ROWS)
        for j in range(nbj):
            lanes = slice(j * BS, (j + 1) * BS)
            flag = live[j]
            for b in range(1, nbi):
                flag = jnp.where(bi == b, live[b * nbj + j], flag)
            ocean = ocean_ref[here, lanes].astype(jnp.float32)
            ice = ice_ref[here, lanes].astype(jnp.float32)
            mass = mass_ref[here, lanes]
            scaled = flag * ocean
            for comp in range(2):
                vel = vel_ref[comp, here, lanes]
                X[comp, j, there, :] = vel
                X[2 + comp, j, there, :] = scaled * (stress_ref[comp, here, lanes] + mass * vel)
            X[DIAG, j, there, :] = ocean * (mass + drag_ref[here, lanes]) + (1.0 - ocean)
            X[5, j, there, :] = scaled * ice * strength_ref[here, lanes]
        return carry

    lax.fori_loop(0, rows // ROWS, local, 0)

    base = PAD + DEPTH
    for side, j in ((0, nbj - 1), (1, 0)):
        shift = DEPTH if side == 0 else 0

        def pack(field, carry, side=side, j=j, shift=shift):
            packed = jnp.zeros((group, BS), jnp.float32)
            for g in range(PACKED):
                x = X[field, j, base + g * group : base + (g + 1) * group, :]
                mine = jnp.logical_and(lane_g >= g * DEPTH, lane_g < (g + 1) * DEPTH)
                packed = jnp.where(mine, turn(x, g * DEPTH + shift), packed)
            PB[side, field] = packed
            return carry

        lax.fori_loop(0, FIELDS, pack, 0)
        for low in range(2):
            first = base + (rows - DEPTH if low else 0)
            packed = jnp.zeros((DEPTH, BS), jnp.float32)
            for field in range(FIELDS):
                x = X[field, j, first : first + DEPTH, :]
                mine = jnp.logical_and(lane >= field * DEPTH, lane < (field + 1) * DEPTH)
                packed = jnp.where(mine, turn(x, field * DEPTH + shift), packed)
            CB[2 * side + low] = packed

    moved = []
    for d, (dr, dc) in enumerate(DIRS):
        if dc == 0:
            first, there = (base, base + rows) if dr < 0 else (base + rows - DEPTH, PAD)
            src = X.at[:, pl.ds(0, nbj), pl.ds(first, DEPTH), :]
            dst = X.at[:, pl.ds(0, nbj), pl.ds(there, DEPTH), :]
        elif dr == 0:
            side = 0 if dc > 0 else 1
            src, dst = PB.at[side], PR.at[side]
        else:
            n = (0 if dc > 0 else 2) + (1 if dr > 0 else 0)
            src, dst = CB.at[n], CR.at[n]
        moved.append(
            pltpu.make_async_remote_copy(
                src_ref=src,
                dst_ref=dst,
                send_sem=send_sem.at[d],
                recv_sem=recv_sem.at[d],
                device_id=device(dr, dc),
                device_id_type=MESH,
            )
        )
    pl.semaphore_wait(barrier, len(partners))
    for d in (2, 5, 0, 1, 3, 4, 6, 7):
        pl.when(exists(*DIRS[d]))(moved[d].start)
    for d in (0, 1, 2, 5, 3, 4, 6, 7):
        dr, dc = DIRS[d]
        pl.when(exists(-dr, -dc))(moved[d].wait_recv)

    for field in range(FIELDS):
        fill = filling(field)
        for j in range(nbj):
            for at, flag in ((PAD, has_n), (base + rows, has_s)):
                X[field, j, at : at + DEPTH, :] = jnp.where(flag, X[field, j, at : at + DEPTH, :], fill)
        for low, at, flag in ((1, PAD, has_n), (0, base + rows, has_s)):
            from_w = turn(CR[low], -(field * DEPTH + DEPTH))
            from_e = turn(CR[2 + low], -(field * DEPTH))
            is_w = jnp.logical_and(lane >= BS - DEPTH, jnp.logical_and(flag, has_w))
            is_e = jnp.logical_and(lane < DEPTH, jnp.logical_and(flag, has_e))
            X[field, nbj, at : at + DEPTH, :] = jnp.where(is_e, from_e, jnp.where(is_w, from_w, fill))

    def unpack(field, carry):
        fill = jnp.where(field == DIAG, 1.0, 0.0)
        w, e = PR[0, field], PR[1, field]
        is_w = jnp.logical_and(lane_g >= BS - DEPTH, has_w)
        is_e = jnp.logical_and(lane_g < DEPTH, has_e)
        for g in range(PACKED):
            from_w = turn(w, -(g * DEPTH + DEPTH))
            from_e = turn(e, -(g * DEPTH))
            X[field, nbj, base + g * group : base + (g + 1) * group, :] = jnp.where(
                is_e, from_e, jnp.where(is_w, from_w, fill)
            )
        return carry

    lax.fori_loop(0, FIELDS, unpack, 0)

    def fold(x):
        total = x[0:8]
        for n in range(1, ROWS // 8):
            total = total + x[8 * n : 8 * n + 8]
        return total

    def sweep_row(t):
        per = per_block * nbi
        shift = 1 + lax.div(t + (per - 1), per)
        for b in range(1, nbi):
            shift = shift + lax.div(t + (per - 1 - b * per_block), per)
        return pl.multiple_of(t * ROWS + PAD * shift, PAD)

    def neighbours(ref, index, j, first):
        return [ref[index + (j, pl.ds(first + d, ROWS))] for d in (-1, 0, 1)]

    def across(es, ws, j, ring):
        if ring:
            right, left = es[(j + 1) % nl], ws[(j - 1) % nl]
        else:
            right, left = 0.0, 0.0
        return jnp.where(last_lane, right, es[j]), jnp.where(first_lane, left, ws[j])

    def setup(t, acc, own):
        start = pl.multiple_of(t * ROWS, ROWS)
        here = pl.ds(start, ROWS)
        inside = pl.ds(pl.multiple_of(PAD + start, PAD), ROWS)
        at = sweep_row(t)
        us = [neighbours(X, (0,), j, PAD + start) for j in range(nl)]
        vs = [neighbours(X, (1,), j, PAD + start) for j in range(nl)]
        eu, wu = [east(x[1]) for x in us], [west(x[1]) for x in us]
        ev, wv = [east(x[1]) for x in vs], [west(x[1]) for x in vs]
        for j in range(nl):
            u_e, u_w = across(eu, wu, j, True)
            v_e, v_w = across(ev, wv, j, True)
            e11 = 0.5 * (us[j][2] - us[j][0])
            e22 = 0.5 * (v_e - v_w)
            e12 = 0.25 * (u_e - u_w + vs[j][2] - vs[j][0])
            deform = 1.25 * (e11 * e11 + e22 * e22) + e12 * e12 + 1.5 * e11 * e22
            zeta = X[5, j, inside, :] / (2.0 * jnp.sqrt(deform + DMIN_SQ))
            total = X[DIAG, j, inside, :] + 3.0 * zeta
            inv = 1.0 / total
            CO[0, j, here, :] = inv
            CO[1, j, here, :] = 0.2 * zeta * inv
            CO[2, j, here, :] = total
            CO[3, j, here, :] = 0.25 * zeta
            for comp in range(2):
                rhs = X[2 + comp, j, inside, :]
                V[0, comp, j, here, :] = rhs
                Z0[comp, j, pl.ds(at, ROWS), :] = rhs * inv
                if own and j < nbj:
                    acc = acc + fold(rhs * rhs)
        return acc

    def put_products(step, values):
        for i, value in enumerate(values):
            n = INDEX[(i, step)]
            GB[n : n + 1, :] = jnp.sum(value, axis=0, keepdims=True)

    GB[COUNT - 1 : COUNT, :] = jnp.zeros((1, BS), jnp.float32)
    for t in (0, chunks - 1):
        setup(t, None, False)
    put_products(0, [lax.fori_loop(1, chunks - 1, lambda t, acc: setup(t, acc, True), zero8)])

    def block_sums(Z, j, at):
        p, q = neighbours(Z, (0,), j, at), neighbours(Z, (1,), j, at)
        sums = []
        for middle, ye, yw in neighbour_sum(p[1], p[0], p[2], q[1], q[0], q[2]):
            sums.append(
                middle + jnp.where(last_lane, 0.0, east(ye)) + jnp.where(first_lane, 0.0, west(yw))
            )
        return (p[1], q[1]), sums

    def sweep(step):
        def first(t, carry):
            at = sweep_row(t)
            here = pl.ds(pl.multiple_of(t * ROWS, ROWS), ROWS)
            for j in range(nl):
                z, sums = block_sums(Z0, j, at)
                k = CO[1, j, here, :]
                for comp in range(2):
                    Z1[comp, j, pl.ds(at, ROWS), :] = z[comp] + k * sums[comp]
            return carry

        def second(t, carry):
            at = sweep_row(t)
            start = pl.multiple_of(t * ROWS, ROWS)
            for j in range(nl):
                z, sums = block_sums(Z1, j, at)
                k = CO[1, j, pl.ds(start, ROWS), :]
                for comp in range(2):
                    z0 = Z0[comp, j, pl.ds(at, ROWS), :]
                    D[step, comp, j, pl.ds(pl.multiple_of(PAD + start, PAD), ROWS), :] = (
                        0.2 * z[comp] + 0.8 * z0 + k * sums[comp]
                    )
            return carry

        lax.fori_loop(0, chunks, first, 0)
        lax.fori_loop(0, chunks, second, 0)

    def operator(step):
        last = step == STEPS - 1

        def body(t, acc, own):
            acc = list(acc)
            at = sweep_row(t)
            start = pl.multiple_of(t * ROWS, ROWS)
            here = pl.ds(start, ROWS)
            z, middle, es, ws = [], [], [[], []], [[], []]
            for j in range(nl):
                p = neighbours(D, (step, 0), j, PAD + start)
                q = neighbours(D, (step, 1), j, PAD + start)
                parts = neighbour_sum(p[1], p[0], p[2], q[1], q[0], q[2])
                z.append((p[1], q[1]))
                middle.append([part[0] for part in parts])
                for comp in range(2):
                    es[comp].append(east(parts[comp][1]))
                    ws[comp].append(west(parts[comp][2]))
            for comp in range(2):
                for j in range(nbj if last else nl):
                    e, w = across(es[comp], ws[comp], j, True)
                    image = CO[2, j, here, :] * z[j][comp] - CO[3, j, here, :] * (middle[j][comp] + e + w)
                    old = V[step, comp, j, here, :]
                    new = image - old
                    if not last:
                        V[step + 1, comp, j, here, :] = new
                        Z0[comp, j, pl.ds(at, ROWS), :] = new * CO[0, j, here, :]
                    if own and j < nbj:
                        for i in range(step + 1):
                            earlier = old if i == step else V[i, comp, j, here, :]
                            acc[i] = acc[i] + fold(new * earlier)
                        acc[step + 1] = acc[step + 1] + fold(new * new)
            return tuple(acc)

        if not last:
            for t in (0, chunks - 1):
                body(t, (), False)
        start = (zero8,) * (step + 2)
        put_products(step + 1, lax.fori_loop(1, chunks - 1, lambda t, acc: body(t, acc, True), start))

    for step in range(STEPS):
        sweep(step)
        operator(step)

    pending = []

    def spread(src, buffer, count, send, recv, along_row):
        out = [
            pltpu.make_async_remote_copy(
                src_ref=src,
                dst_ref=buffer.at[o - 1],
                send_sem=send.at[o - 1],
                recv_sem=recv.at[o - 1],
                device_id=device(o, 0) if along_row else device(0, o),
                device_id_type=MESH,
            )
            for o in range(1, count)
        ]
        for copy in out:
            copy.start()
        for copy in out:
            copy.wait_recv()
        pending.extend(out)
        total = src[...]
        for o in range(1, count):
            total = total + buffer[o - 1]
        return total

    GX[...] = spread(GB, R1, n_row, s1, r1, True)
    products = jnp.sum(spread(GX, R2, n_col, s2, r2, False), axis=1, keepdims=True)
    weights = scalars([products[n : n + 1] for n in range(len(PAIRS))])

    for comp in range(2):
        for j in range(nbj):
            total = None
            for step in range(STEPS):
                term = weights[step] * D[step, comp, j, base : base + rows, :]
                total = term if total is None else total + term
            out_ref[comp, :, j * BS : (j + 1) * BS] = total
    for d, (dr, dc) in enumerate(DIRS):
        pl.when(exists(dr, dc))(moved[d].wait_send)
    for copy in pending:
        copy.wait_send()


def solution(mesh):
    n_chip, n_row, n_grp = mesh.shape["chip"], mesh.shape["row"], mesh.shape["grp"]

    def shards(old_velocity, surface_stress, mass_term, ocean_drag, strength, ice_mask, ocean_mask, ice_blocks):
        _, rows, cols = old_velocity.shape
        nbi, nbj = rows // BS, cols // BS
        nl, long = nbj + 1, rows + 2 * DEPTH
        vmem = pl.BlockSpec(memory_space=pltpu.VMEM)
        f32 = jnp.float32
        n_col = n_chip * n_grp
        dma = pltpu.SemaphoreType.DMA
        return pl.pallas_call(
            functools.partial(kernel, (n_chip, n_row, n_grp, rows, cols)),
            out_shape=jax.ShapeDtypeStruct(old_velocity.shape, f32),
            in_specs=[pl.BlockSpec(memory_space=pl.ANY)] * 7 + [pl.BlockSpec(memory_space=pltpu.SMEM)],
            out_specs=vmem,
            scratch_shapes=[
                pltpu.VMEM(old_velocity.shape, f32),
                pltpu.VMEM(old_velocity.shape, f32),
                pltpu.VMEM((rows, cols), f32),
                pltpu.VMEM((rows, cols), f32),
                pltpu.VMEM((rows, cols), f32),
                pltpu.VMEM((rows, cols), jnp.int32),
                pltpu.VMEM((rows, cols), jnp.int32),
                pltpu.VMEM((FIELDS, nl, long + 2 * PAD, BS), f32),
                pltpu.VMEM((STEPS, 2, nl, long + 2 * PAD, BS), f32),
                pltpu.VMEM((STEPS, 2, nl, long, BS), f32),
                pltpu.VMEM((2, nl, long + (nbi + 3) * PAD, BS), f32),
                pltpu.VMEM((2, nl, long + (nbi + 3) * PAD, BS), f32),
                pltpu.VMEM((4, nl, long, BS), f32),
                pltpu.VMEM((2, FIELDS, rows // PACKED, BS), f32),
                pltpu.VMEM((2, FIELDS, rows // PACKED, BS), f32),
                pltpu.VMEM((4, DEPTH, BS), f32),
                pltpu.VMEM((4, DEPTH, BS), f32),
                pltpu.VMEM((COUNT, BS), f32),
                pltpu.VMEM((COUNT, BS), f32),
                pltpu.VMEM((n_row - 1, COUNT, BS), f32),
                pltpu.VMEM((n_col - 1, COUNT, BS), f32),
                dma((7,)),
                dma((len(DIRS),)),
                dma((len(DIRS),)),
                dma((n_row - 1,)),
                dma((n_row - 1,)),
                dma((n_col - 1,)),
                dma((n_col - 1,)),
            ],
            compiler_params=pltpu.CompilerParams(
                collective_id=0, has_side_effects=True, vmem_limit_bytes=60 * 1024 * 1024
            ),
        )(old_velocity, surface_stress, mass_term, ocean_drag, strength, ice_mask, ocean_mask, ice_blocks)

    return jax.shard_map(
        shards,
        mesh=mesh,
        in_specs=(
            P(None, "row", ("chip", "grp")),
            P(None, "row", ("chip", "grp")),
            P("row", ("chip", "grp")),
            P("row", ("chip", "grp")),
            P("row", ("chip", "grp")),
            P("row", ("chip", "grp")),
            P("row", ("chip", "grp")),
            P(("chip", "grp"), None),
        ),
        out_specs=P(None, "row", ("chip", "grp")),
        check_vma=False,
    )
```

time: 58.8 us -> 49.7 us (0.85)
  local copies, waits for them, and re-layouts: 8.28 us -> 1.87 us
  Pallas kernels: 50.1 us -> 47.6 us
    unnamed x17 -> x1, local copies, waits for them, and re-layouts: 8.28 us -> 1.87 us
    pallas_call x1, Pallas kernels: 50.1 us -> 47.6 us  [shards(): pl.pallas_call(functools.partial(kernel, (n_chip, n_row, n_grp, rows, col...]
where the time goes in v2:
time: 49.7 us; the launch traced here: 49.5 us
  Pallas kernels  47.6 us (96%)
  local copies, waits for them, and re-layouts  1.87 us (4%)
    pallas_call x1, Pallas kernels, shards(): pl.pallas_call(functools.partial(kernel, (n_chip, n_row, n_grp, rows, col...  47.6 us
    unnamed x1, local copies, waits for them, and re-layouts  1.87 us

profile of v2, /device:TPU:0, one launch (start us, length us, event | category | flops | bytes accessed | tf_op | source)
XLA Modules:
  0.0 49.5 jit_solution(13519991834693962382)
XLA Ops:
  0.0 47.6 %shard_map.82 = f32[2,256,256]{2,1,0:T(8,128)} custom-call(f32[2,256,256]{2,1,0:T(8,128)} %vel_hbm.1, f32[2,256,256]{2,1,0:T(8,128)} %stress_hbm.1, f32[256,256]{1,0:T(8,128)} %mass_hbm.1, f32[256,256]{1,0:T(8,128)} %drag_hbm.1, f32[256,256]{1,0:T(8,128)} %strength_hbm.1, s32[256,256]{1,0:T(8,128)} %ice_hbm.1, s32[256,256]{1,0:T(8,128)} %ocean_hbm.1, ...), custom_call_target="tpu_custom_call" | custom-call | tf_op jit(solution)/shard_map/pallas_call | solution.py:523
  47.6 1.9 %copy.10 = f32[2,256,256]{2,1,0:T(8,128)} copy(f32[2,256,256]{2,1,0:T(8,128)} %shard_map.82) | data formatting | bytes 1048576

commit v3 on v2

--- a/solution.py
+++ b/solution.py
@@ -21,6 +21,10 @@
 PAIRS = [(i, j) for j in range(STEPS + 1) for i in range(j + 1)]
 INDEX = {pair: n for n, pair in enumerate(PAIRS)}
 COUNT = 16
+UNROLL_LOCAL = 16
+UNROLL_SETUP = 16
+UNROLL_SWEEP = 18
+UNROLL_OPERATOR = 16
 
 
 def neighbour_sum(p, p_n, p_s, q, q_n, q_s):
@@ -28,6 +32,28 @@
     tp = p_s - p_n
     q5 = 5.0 * q
     return (5.0 * (p_n + p_s), p + tq, p - tq), (q_n + q_s, q5 + tp, q5 - tp)
+
+
+def aligned(index, multiple):
+    return index if isinstance(index, int) else pl.multiple_of(index, multiple)
+
+
+def chunked(low, high, unroll, body, carry):
+    count = high - low
+    if count <= unroll:
+        for t in range(low, high):
+            carry = body(t, carry)
+        return carry
+
+    def several(n, carry):
+        for i in range(unroll):
+            carry = body(low + n * unroll + i, carry)
+        return carry
+
+    carry = lax.fori_loop(0, count // unroll, several, carry)
+    for t in range(low + count // unroll * unroll, high):
+        carry = body(t, carry)
+    return carry
 
 
 def scalars(gram):
@@ -222,10 +248,10 @@
         load.wait()
 
     def local(t, carry):
-        bi = lax.div(t, per_block)
-        start = pl.multiple_of(t * ROWS, ROWS)
+        bi = t // per_block if isinstance(t, int) else lax.div(t, per_block)
+        start = aligned(t * ROWS, ROWS)
         here = pl.ds(start, ROWS)
-        there = pl.ds(pl.multiple_of(PAD + DEPTH + start, PAD), ROWS)
+        there = pl.ds(aligned(PAD + DEPTH + start, PAD), ROWS)
         for j in range(nbj):
             lanes = slice(j * BS, (j + 1) * BS)
             flag = live[j]
@@ -243,7 +269,7 @@
             X[5, j, there, :] = scaled * ice * strength_ref[here, lanes]
         return carry
 
-    lax.fori_loop(0, rows // ROWS, local, 0)
+    chunked(0, rows // ROWS, UNROLL_LOCAL, local, 0)
 
     base = PAD + DEPTH
     for side, j in ((0, nbj - 1), (1, 0)):
@@ -332,10 +358,12 @@
 
     def sweep_row(t):
         per = per_block * nbi
-        shift = 1 + lax.div(t + (per - 1), per)
-        for b in range(1, nbi):
+        if isinstance(t, int):
+            return t * ROWS + PAD * (1 + sum((t + per - 1 - b * per_block) // per for b in range(nbi)))
+        shift = 1
+        for b in range(nbi):
             shift = shift + lax.div(t + (per - 1 - b * per_block), per)
-        return pl.multiple_of(t * ROWS + PAD * shift, PAD)
+        return aligned(t * ROWS + PAD * shift, PAD)
 
     def neighbours(ref, index, j, first):
         return [ref[index + (j, pl.ds(first + d, ROWS))] for d in (-1, 0, 1)]
@@ -348,9 +376,9 @@
         return jnp.where(last_lane, right, es[j]), jnp.where(first_lane, left, ws[j])
 
     def setup(t, acc, own):
-        start = pl.multiple_of(t * ROWS, ROWS)
+        start = aligned(t * ROWS, ROWS)
         here = pl.ds(start, ROWS)
-        inside = pl.ds(pl.multiple_of(PAD + start, PAD), ROWS)
+        inside = pl.ds(aligned(PAD + start, PAD), ROWS)
         at = sweep_row(t)
         us = [neighbours(X, (0,), j, PAD + start) for j in range(nl)]
         vs = [neighbours(X, (1,), j, PAD + start) for j in range(nl)]
@@ -386,7 +414,7 @@
     GB[COUNT - 1 : COUNT, :] = jnp.zeros((1, BS), jnp.float32)
     for t in (0, chunks - 1):
         setup(t, None, False)
-    put_products(0, [lax.fori_loop(1, chunks - 1, lambda t, acc: setup(t, acc, True), zero8)])
+    put_products(0, [chunked(1, chunks - 1, UNROLL_SETUP, lambda t, acc: setup(t, acc, True), zero8)])
 
     def block_sums(Z, j, at):
         p, q = neighbours(Z, (0,), j, at), neighbours(Z, (1,), j, at)
@@ -400,7 +428,7 @@
     def sweep(step):
         def first(t, carry):
             at = sweep_row(t)
-            here = pl.ds(pl.multiple_of(t * ROWS, ROWS), ROWS)
+            here = pl.ds(aligned(t * ROWS, ROWS), ROWS)
             for j in range(nl):
                 z, sums = block_sums(Z0, j, at)
                 k = CO[1, j, here, :]
@@ -410,19 +438,19 @@
 
         def second(t, carry):
             at = sweep_row(t)
-            start = pl.multiple_of(t * ROWS, ROWS)
+            start = aligned(t * ROWS, ROWS)
             for j in range(nl):
                 z, sums = block_sums(Z1, j, at)
                 k = CO[1, j, pl.ds(start, ROWS), :]
                 for comp in range(2):
                     z0 = Z0[comp, j, pl.ds(at, ROWS), :]
-                    D[step, comp, j, pl.ds(pl.multiple_of(PAD + start, PAD), ROWS), :] = (
+                    D[step, comp, j, pl.ds(aligned(PAD + start, PAD), ROWS), :] = (
                         0.2 * z[comp] + 0.8 * z0 + k * sums[comp]
                     )
             return carry
 
-        lax.fori_loop(0, chunks, first, 0)
-        lax.fori_loop(0, chunks, second, 0)
+        chunked(0, chunks, UNROLL_SWEEP, first, 0)
+        chunked(0, chunks, UNROLL_SWEEP, second, 0)
 
     def operator(step):
         last = step == STEPS - 1
@@ -430,7 +458,7 @@
         def body(t, acc, own):
             acc = list(acc)
             at = sweep_row(t)
-            start = pl.multiple_of(t * ROWS, ROWS)
+            start = aligned(t * ROWS, ROWS)
             here = pl.ds(start, ROWS)
             z, middle, es, ws = [], [], [[], []], [[], []]
             for j in range(nl):
@@ -462,7 +490,7 @@
             for t in (0, chunks - 1):
                 body(t, (), False)
         start = (zero8,) * (step + 2)
-        put_products(step + 1, lax.fori_loop(1, chunks - 1, lambda t, acc: body(t, acc, True), start))
+        put_products(step + 1, chunked(1, chunks - 1, UNROLL_OPERATOR, lambda t, acc: body(t, acc, True), start))
 
     for step in range(STEPS):
         sweep(step)

time: 49.7 us -> 32.5 us (0.65)
  Pallas kernels: 47.6 us -> 30.5 us
    pallas_call x1, Pallas kernels: 47.6 us -> 30.5 us  [shards(): pl.pallas_call(functools.partial(kernel, (n_chip, n_row, n_grp, rows, col...]
where the time goes in v3:
time: 32.5 us; the launch traced here: 32.3 us
  Pallas kernels  30.5 us (94%)
  local copies, waits for them, and re-layouts  1.87 us (6%)
    pallas_call x1, Pallas kernels, shards(): pl.pallas_call(functools.partial(kernel, (n_chip, n_row, n_grp, rows, col...  30.5 us
    unnamed x1, local copies, waits for them, and re-layouts  1.87 us

profile of v3, /device:TPU:0, one launch (start us, length us, event | category | flops | bytes accessed | tf_op | source)
XLA Modules:
  0.0 32.3 jit_solution(11253429250798158742)
XLA Ops:
  0.0 30.5 %shard_map.82 = f32[2,256,256]{2,1,0:T(8,128)} custom-call(f32[2,256,256]{2,1,0:T(8,128)} %vel_hbm.1, f32[2,256,256]{2,1,0:T(8,128)} %stress_hbm.1, f32[256,256]{1,0:T(8,128)} %mass_hbm.1, f32[256,256]{1,0:T(8,128)} %drag_hbm.1, f32[256,256]{1,0:T(8,128)} %strength_hbm.1, s32[256,256]{1,0:T(8,128)} %ice_hbm.1, s32[256,256]{1,0:T(8,128)} %ocean_hbm.1, ...), custom_call_target="tpu_custom_call" | custom-call | tf_op jit(solution)/shard_map/pallas_call | solution.py:551
  30.5 1.9 %copy.10 = f32[2,256,256]{2,1,0:T(8,128)} copy(f32[2,256,256]{2,1,0:T(8,128)} %shard_map.82) | data formatting | bytes 1048576
